TPU v7x, 32 devices: a whole 2x2x4 slice. The times are simulated.
32 devices in a mesh: dp: 2 (over x), inblk: 4 (over z), outcol: 4 (over y, core).
Axes of the slice: x: 2, y: 2, z: 4, core: 2. Of those that a mesh axis runs over, the one named last changes fastest.
Arguments:
- activations: bfloat16 [256, 8192], P('dp', ('inblk', 'outcol')), may hold values from -1.5 to 1.5
- cotangent: bfloat16 [256, 1024], P('dp', 'outcol'), may hold values from -6 to 6
- base_weight: bfloat16 [8192, 1024], P('inblk', 'outcol'), may hold values from -0.09375 to 0.09375
- skew_param: float32 [32, 256, 256], P(('inblk', 'outcol'), 'dp'), may hold values from -0.3125 to 0.3125
Outputs:
- grad_acts: bfloat16 [256, 8192], P('dp', ('inblk', 'outcol'))
- grad_skew: float32 [32, 256, 256], P(('inblk', 'outcol'), 'dp')
All inputs are finite; a program needn't handle non-finite values.
Results may differ from a plain program's by a relative error of at most 0.0058.
Values may be sent and summed in bfloat16 or wider, within the bound.
A program may use at most 64 MiB of HBM per device.

v0:
```python
import functools

import jax
import jax.numpy as jnp
from jax import lax
from jax.experimental import pallas as pl
from jax.experimental.pallas import tpu as pltpu
from jax.sharding import PartitionSpec as P

F32, BF16 = jnp.float32, jnp.bfloat16
MESH = pl.DeviceIdType.MESH


def mm(left, right):
    return jnp.dot(left, right, preferred_element_type=F32)


def halves(value):
    high = value.astype(BF16)
    return high, (value - high.astype(F32)).astype(BF16)


def mm3(left, right):
    return mm(left[0], right[0]) + (mm(left[0], right[1]) + mm(left[1], right[0]))


def chain(grad, mats, index):
    grad_b = grad.astype(BF16)
    x = mm(mats[index, 0], grad_b) + mm(grad_b, mats[index, 0])
    x_b = x.astype(BF16)
    kx = (x + mm(mats[index, 3], x_b)).astype(BF16)
    lead = 2.0 * grad + x
    dq = (lead + x) + mm(mats[index, 4], x_b)
    dq = dq + mm(lead.astype(BF16), mats[index, 2]) + mm(kx, mats[index, 1])
    return dq - dq.T


def exchange(n_dp, act_hbm, cot_hbm, w_hbm, skew_hbm, ga_ref, gs_ref, mats, act_t, feat,
             skew_own, skew_all, act_all, cot_v, w_v,
             s1_send, s1_recv, part, y_send, y_recv, dq_v,
             loc, skew_s, skew_r, act_s, act_r, s1_s, s1_r, y_s, y_r, f_s, f_r):
    me, out = lax.axis_index("dp"), lax.axis_index("outcol")
    side, core = lax.div(out, 2), lax.rem(out, 2)
    sib = side * 2 + 1 - core
    far = (1 - side) * 2 + core
    far_sib = (1 - side) * 2 + 1 - core
    tokens = cot_v.shape[0]
    blocks, rows, width = skew_own.shape
    peers = [lax.rem(me + step, n_dp) for step in range(1, n_dp)]

    loads = [
        pltpu.make_async_copy(src, dst, loc.at[i])
        for i, (src, dst) in enumerate(
            ((cot_hbm, cot_v), (w_hbm, w_v), (skew_hbm, skew_own), (act_hbm, act_all.at[0]))
        )
    ]
    for load in loads:
        load.start()

    barrier = pltpu.get_barrier_semaphore()
    pl.semaphore_signal(barrier, inc=1, device_id={"outcol": sib}, device_id_type=MESH)
    pl.semaphore_signal(barrier, inc=1, device_id={"outcol": far}, device_id_type=MESH)
    for peer in peers:
        pl.semaphore_signal(barrier, inc=1, device_id={"dp": peer}, device_id_type=MESH)

    def partial_of(owner, block):
        start = pl.multiple_of((owner * blocks + block) * width, width)
        return lax.dot_general(
            cot_v[...], w_v[pl.ds(start, width), :], (((1,), (1,)), ((), ())),
            preferred_element_type=F32,
        )

    def remote(src, dst, send, recv, **where):
        return pltpu.make_async_remote_copy(
            src_ref=src, dst_ref=dst, send_sem=send, recv_sem=recv,
            device_id=where, device_id_type=MESH,
        )

    loads[2].wait()
    skew_all[me] = skew_own[...].astype(skew_all.dtype)
    loads[0].wait()
    loads[1].wait()
    for block in range(blocks):
        s1_send[block, 0] = partial_of(sib, block).astype(BF16)
        s1_send[block, 1] = partial_of(far_sib, block).astype(BF16)

    pl.semaphore_wait(barrier, 1 + n_dp)

    s1 = [remote(s1_send.at[b], s1_recv.at[b], s1_s.at[b], s1_r.at[b], outcol=sib)
          for b in range(blocks)]
    skews = [remote(skew_all.at[me], skew_all.at[me], skew_s.at[i], skew_r.at[i], dp=peer)
             for i, peer in enumerate(peers)]
    acts = [remote(act_hbm, act_all.at[i + 1], act_s.at[i], act_r.at[i], dp=peer)
            for i, peer in enumerate(peers)]
    for copy in s1 + skews + acts:
        copy.start()

    for block in range(blocks):
        part[block, 0] = partial_of(out, block)
        part[block, 1] = partial_of(far, block)

    sides = [remote(y_send.at[b], y_recv.at[b], y_s.at[b], y_r.at[b], outcol=far)
             for b in range(blocks)]
    for block in range(blocks):
        s1[block].wait_recv()
        y_send[block] = (part[block, 1] + s1_recv[block, 1].astype(F32)).astype(BF16)
        sides[block].start()
    loads[3].wait()
    act_t[:, :tokens] = act_all[0].T
    feats = []
    for block in range(blocks):
        sides[block].wait_recv()
        total = part[block, 0] + s1_recv[block, 0].astype(F32) + y_recv[block].astype(F32)
        feat[block, 0] = total.astype(BF16)
        for i, peer in enumerate(peers):
            copy = remote(feat.at[block, 0], feat.at[block, i + 1],
                          f_s.at[block, i], f_r.at[block, i], dp=peer)
            copy.start()
            feats.append(copy)

    for copy in skews:
        copy.wait_recv()
    eye = (lax.broadcasted_iota(jnp.int32, (width, width), 0)
           == lax.broadcasted_iota(jnp.int32, (width, width), 1)).astype(F32)
    for block in range(blocks):
        given = skew_all[:, block].reshape(width, width).astype(F32)
        m1 = given.T - given
        m1_h = halves(m1)
        m2 = mm3(m1_h, m1_h)
        m2_h = halves(m2)
        m4 = mm3(m2_h, m2_h)
        k0 = 2.0 * m1 + m2
        k0_h = halves(k0)
        c2 = mm3(k0_h, m2_h)
        c4 = mm3(k0_h, halves(m4))
        n0 = m2 + m4
        rot_t = (eye + ((k0 + n0) + (c2 + c4))).astype(BF16)
        ga_ref[:, block * width:(block + 1) * width] = mm(feat[block, 0], rot_t).astype(BF16)
        mats[block, 0] = m1_h[0]
        mats[block, 1] = m2_h[0]
        mats[block, 2] = n0.astype(BF16)
        mats[block, 3] = k0_h[0]
        mats[block, 4] = (k0 + m2 + c2).astype(BF16)

    for slot in range(1, n_dp):
        acts[slot - 1].wait_recv()
        act_t[:, slot * tokens:(slot + 1) * tokens] = act_all[slot].T

    for block in range(blocks):
        for copy in feats[block * (n_dp - 1):(block + 1) * (n_dp - 1)]:
            copy.wait_recv()
        if block < blocks - 1:
            grad = mm(act_t[block * width:(block + 1) * width, :],
                      feat[block].reshape(n_dp * tokens, width))
            dq_v[...] = chain(grad, mats, block)
            gs_ref[block] = dq_v[pl.ds(pl.multiple_of(me * rows, rows), rows), :]

    for copy in s1 + skews + acts + sides + feats:
        copy.wait_send()


def finish(n_dp, ga_ref, gs_ref, mats, act_t, feat, ga_out, gs_out, dq_v, sems):
    me = lax.axis_index("dp")
    blocks, rows, width = gs_out.shape
    last = blocks - 1
    writes = [pltpu.make_async_copy(ga_ref, ga_out, sems.at[0])]
    writes += [pltpu.make_async_copy(gs_ref.at[b], gs_out.at[b], sems.at[b + 1])
               for b in range(last)]
    for write in writes:
        write.start()
    grad = mm(act_t[last * width:, :], feat[last].reshape(-1, width))
    dq_v[...] = chain(grad, mats, last)
    end = pltpu.make_async_copy(dq_v.at[pl.ds(pl.multiple_of(me * rows, rows), rows)],
                                gs_out.at[last], sems.at[blocks])
    end.start()
    for write in writes + [end]:
        write.wait()


def body(n_dp, activations, cotangent, base_weight, skew_param):
    tokens, own = activations.shape
    blocks, rows, width = skew_param.shape
    wire = BF16 if rows % 16 == 0 else F32
    dma = pltpu.SemaphoreType.DMA
    vmem = pl.BlockSpec(memory_space=pltpu.VMEM)
    outs = (jax.ShapeDtypeStruct((tokens, own), BF16),
            jax.ShapeDtypeStruct((blocks, rows, width), F32))
    activations, cotangent, base_weight, skew_param = (
        pltpu.with_memory_space_constraint(each, pltpu.HBM)
        for each in (activations, cotangent, base_weight, skew_param))
    parts = pl.pallas_call(
        functools.partial(exchange, n_dp),
        out_shape=(outs[0],
                   jax.ShapeDtypeStruct((blocks - 1, rows, width), F32),
                   jax.ShapeDtypeStruct((blocks, 5, width, width), BF16),
                   jax.ShapeDtypeStruct((own, n_dp * tokens), BF16),
                   jax.ShapeDtypeStruct((blocks, n_dp, tokens, width), BF16)),
        in_specs=[pl.BlockSpec(memory_space=pltpu.HBM)] * 4,
        out_specs=[vmem] * 5,
        scratch_shapes=[
            pltpu.VMEM((blocks, rows, width), F32),
            pltpu.VMEM((n_dp, blocks, rows, width), wire),
            pltpu.VMEM((n_dp, tokens, own), BF16),
            pltpu.VMEM(cotangent.shape, BF16),
            pltpu.VMEM(base_weight.shape, BF16),
            pltpu.VMEM((blocks, 2, tokens, width), BF16),
            pltpu.VMEM((blocks, 2, tokens, width), BF16),
            pltpu.VMEM((blocks, 2, tokens, width), F32),
            pltpu.VMEM((blocks, tokens, width), BF16),
            pltpu.VMEM((blocks, tokens, width), BF16),
            pltpu.VMEM((width, width), F32),
            dma((4,)),
            dma((n_dp - 1,)), dma((n_dp - 1,)),
            dma((n_dp - 1,)), dma((n_dp - 1,)),
            dma((blocks,)), dma((blocks,)),
            dma((blocks,)), dma((blocks,)),
            dma((blocks, n_dp - 1)), dma((blocks, n_dp - 1)),
        ],
        compiler_params=pltpu.CompilerParams(
            collective_id=0, has_side_effects=True, vmem_limit_bytes=32 * 2**20),
    )(activations, cotangent, base_weight, skew_param)
    return tuple(pl.pallas_call(
        functools.partial(finish, n_dp),
        out_shape=outs,
        in_specs=[vmem] * 5,
        out_specs=[pl.BlockSpec(memory_space=pltpu.HBM)] * 2,
        scratch_shapes=[pltpu.VMEM((width, width), F32), dma((blocks + 1,))],
        compiler_params=pltpu.CompilerParams(vmem_limit_bytes=32 * 2**20),
    )(*parts))


def solution(mesh):
    return jax.shard_map(
        functools.partial(body, mesh.shape["dp"]),
        mesh=mesh,
        in_specs=(
            P("dp", ("inblk", "outcol")),
            P("dp", "outcol"),
            P("inblk", "outcol"),
            P(("inblk", "outcol"), "dp", None),
        ),
        out_specs=(P("dp", ("inblk", "outcol")), P(("inblk", "outcol"), "dp", None)),
        check_vma=False,
    )
```

profile of v0, /device:TPU:0, one launch (start us, length us, event | category | flops | bytes accessed | tf_op | source)
XLA Modules:
  0.0 16.1 jit_solution(11326065006135395357)
XLA Ops:
  0.6 13.9 %shard_map.59 = (bf16[128,512]{1,0:T(8,128)(2,1)S(1)}, f32[1,128,256]{2,1,0:T(8,128)S(1)}, bf16[2,5,256,256]{3,2,1,0:T(8,128)(2,1)S(1)}, bf16[512,256]{1,0:T(8,128)(2,1)S(1)}, bf16[2,2,128,256]{3,2,1,0:T(8,128)(2,1)S(1)}) custom-call(bf16[128,512]{1,0:T(8,128)(2,1)} %act_hbm.1, bf16[128,256]{1,0:T(8,128)(2,1)} %cot_hbm.1, bf16[2048,256]{1,0:T(8,128)(2,1)} %w_hbm.1, ...), custom_call_target="tpu_custom_call" | custom-call | tf_op jit(solution)/shard_map/pallas_call | solution.py:191
  14.6 1.5 %shard_map.60 = (bf16[128,512]{1,0:T(8,128)(2,1)}, f32[2,128,256]{2,1,0:T(8,128)}) custom-call(bf16[128,512]{1,0:T(8,128)(2,1)S(1)} %get-tuple-element.7.ga_ref, f32[1,128,256]{2,1,0:T(8,128)S(1)} %get-tuple-element.8.gs_ref, bf16[2,5,256,256]{3,2,1,0:T(8,128)(2,1)S(1)} %get-tuple-element.9.mats, bf16[512,256]{1,0:T(8,128)(2,1)S(1)} %get-tuple-element.10.act_t, ...), custom_call_target="tpu_custom_call" | custom-call | tf_op jit(solution)/shard_map/pallas_call | solution.py:222
where the time goes:
time: 16.3 us; the launch traced here: 16.1 us
  Pallas kernels  15.5 us (95%)
  between operations  0.64 us (4%)
    pallas_call x1, Pallas kernels, body(): pl.pallas_call(functools.partial(exchange, n_dp), out_shape=(outs[0], jax...  13.9 us
    pallas_call x1, Pallas kernels, body(): pl.pallas_call(functools.partial(finish, n_dp), out_shape=outs, in_specs=...  1.53 us

commit v1 on v0

--- a/solution.py
+++ b/solution.py
@@ -37,7 +37,7 @@
 
 def exchange(n_dp, act_hbm, cot_hbm, w_hbm, skew_hbm, ga_ref, gs_ref, mats, act_t, feat,
              skew_own, skew_all, act_all, cot_v, w_v,
-             s1_send, s1_recv, part, y_send, y_recv, dq_v,
+             s1_send, s1_recv, part, y_send, y_recv, rot_t, dq_v,
              loc, skew_s, skew_r, act_s, act_r, s1_s, s1_r, y_s, y_r, f_s, f_r):
     me, out = lax.axis_index("dp"), lax.axis_index("outcol")
     side, core = lax.div(out, 2), lax.rem(out, 2)
@@ -107,21 +107,11 @@
         sides[block].start()
     loads[3].wait()
     act_t[:, :tokens] = act_all[0].T
-    feats = []
-    for block in range(blocks):
-        sides[block].wait_recv()
-        total = part[block, 0] + s1_recv[block, 0].astype(F32) + y_recv[block].astype(F32)
-        feat[block, 0] = total.astype(BF16)
-        for i, peer in enumerate(peers):
-            copy = remote(feat.at[block, 0], feat.at[block, i + 1],
-                          f_s.at[block, i], f_r.at[block, i], dp=peer)
-            copy.start()
-            feats.append(copy)
-
     for copy in skews:
         copy.wait_recv()
     eye = (lax.broadcasted_iota(jnp.int32, (width, width), 0)
            == lax.broadcasted_iota(jnp.int32, (width, width), 1)).astype(F32)
+    feats = []
     for block in range(blocks):
         given = skew_all[:, block].reshape(width, width).astype(F32)
         m1 = given.T - given
@@ -134,13 +124,24 @@
         c2 = mm3(k0_h, m2_h)
         c4 = mm3(k0_h, halves(m4))
         n0 = m2 + m4
-        rot_t = (eye + ((k0 + n0) + (c2 + c4))).astype(BF16)
-        ga_ref[:, block * width:(block + 1) * width] = mm(feat[block, 0], rot_t).astype(BF16)
+        rot_t[block] = (eye + ((k0 + n0) + (c2 + c4))).astype(BF16)
         mats[block, 0] = m1_h[0]
         mats[block, 1] = m2_h[0]
         mats[block, 2] = n0.astype(BF16)
         mats[block, 3] = k0_h[0]
         mats[block, 4] = (k0 + m2 + c2).astype(BF16)
+
+        sides[block].wait_recv()
+        total = part[block, 0] + s1_recv[block, 0].astype(F32) + y_recv[block].astype(F32)
+        feat[block, 0] = total.astype(BF16)
+        for i, peer in enumerate(peers):
+            copy = remote(feat.at[block, 0], feat.at[block, i + 1],
+                          f_s.at[block, i], f_r.at[block, i], dp=peer)
+            copy.start()
+            feats.append(copy)
+    for block in range(blocks):
+        ga_ref[:, block * width:(block + 1) * width] = mm(
+            feat[block, 0], rot_t[block]).astype(BF16)
 
     for slot in range(1, n_dp):
         acts[slot - 1].wait_recv()
@@ -208,6 +209,7 @@
             pltpu.VMEM((blocks, 2, tokens, width), F32),
             pltpu.VMEM((blocks, tokens, width), BF16),
             pltpu.VMEM((blocks, tokens, width), BF16),
+            pltpu.VMEM((blocks, width, width), BF16),
             pltpu.VMEM((width, width), F32),
             dma((4,)),
             dma((n_dp - 1,)), dma((n_dp - 1,)),

time: 16.3 us -> 16.8 us (1.031)
  Pallas kernels: 15.5 us -> 16 us
    pallas_call x1, Pallas kernels: 13.9 us -> 14.5 us  [body(): pl.pallas_call(functools.partial(exchange, n_dp), out_shape=(outs[0], jax...]
where the time goes in v1:
time: 16.8 us; the launch traced here: 16.6 us
  Pallas kernels  16 us (95%)
  between operations  0.64 us (4%)
    pallas_call x1, Pallas kernels, body(): pl.pallas_call(functools.partial(exchange, n_dp), out_shape=(outs[0], jax...  14.5 us
    pallas_call x1, Pallas kernels, body(): pl.pallas_call(functools.partial(finish, n_dp), out_shape=outs, in_specs=...  1.52 us

profile of v1, /device:TPU:0, one launch (start us, length us, event | category | flops | bytes accessed | tf_op | source)
XLA Modules:
  0.0 16.6 jit_solution(12249935484862550233)
XLA Ops:
  0.6 14.5 %shard_map.59 = (bf16[128,512]{1,0:T(8,128)(2,1)S(1)}, f32[1,128,256]{2,1,0:T(8,128)S(1)}, bf16[2,5,256,256]{3,2,1,0:T(8,128)(2,1)S(1)}, bf16[512,256]{1,0:T(8,128)(2,1)S(1)}, bf16[2,2,128,256]{3,2,1,0:T(8,128)(2,1)S(1)}) custom-call(bf16[128,512]{1,0:T(8,128)(2,1)} %act_hbm.1, bf16[128,256]{1,0:T(8,128)(2,1)} %cot_hbm.1, bf16[2048,256]{1,0:T(8,128)(2,1)} %w_hbm.1, ...), custom_call_target="tpu_custom_call" | custom-call | tf_op jit(solution)/shard_map/pallas_call | solution.py:192
  15.1 1.5 %shard_map.60 = (bf16[128,512]{1,0:T(8,128)(2,1)}, f32[2,128,256]{2,1,0:T(8,128)}) custom-call(bf16[128,512]{1,0:T(8,128)(2,1)S(1)} %get-tuple-element.7.ga_ref, f32[1,128,256]{2,1,0:T(8,128)S(1)} %get-tuple-element.8.gs_ref, bf16[2,5,256,256]{3,2,1,0:T(8,128)(2,1)S(1)} %get-tuple-element.9.mats, bf16[512,256]{1,0:T(8,128)(2,1)S(1)} %get-tuple-element.10.act_t, ...), custom_call_target="tpu_custom_call" | custom-call | tf_op jit(solution)/shard_map/pallas_call | solution.py:224
